TPU v7x, 32 devices: a whole 2x2x4 slice. The times are simulated.
32 devices in a mesh: section: 4 (over x, core), dp: 8 (over z, y).
Axes of the slice: x: 2, y: 2, z: 4, core: 2. Of those that a mesh axis runs over, the one named last changes fastest.
Arguments:
- micro_inputs: bfloat16 [4, 512, 4096], P(None, 'dp'), may hold values from -6 to 6
- out_cotangent: bfloat16 [4, 512, 4096], P(None, 'dp'), may hold values from -0.3125 to 0.3125
- weight_a: bfloat16 [2, 4, 4096, 512], P(None, 'section'), may hold values from -0.09375 to 0.09375
- weight_b: bfloat16 [2, 4, 512, 4096], P(None, 'section'), may hold values from -0.25 to 0.25
- mask_a: int32 [2, 4, 64, 8], P(None, 'section'), may hold values from 0 to 1, as said below
- mask_b: int32 [2, 4, 8, 64], P(None, 'section'), may hold values from 0 to 1, as said below
Outputs:
- grad_a: float32 [2, 4, 4096, 512], P(None, 'section', 'dp')
- grad_b: float32 [2, 4, 512, 4096], P(None, 'section', None, 'dp')
Inputs may be any that keep to these rules, and one draw needn't show every extreme that they name: Each block of a layer is kept with a probability drawn for that layer from 30 to 50 percent; mask_a and mask_b of one layer share it. `mask_b`: drawn with the same per-layer probabilities as mask_a.
All inputs are finite; a program needn't handle non-finite values.
Results may differ from a plain program's by a relative error of at most 0.033.
Values may be sent and summed in bfloat16 or wider, within the bound.
A program may use at most 192 MiB of HBM per device.

v0:
```python
import functools

import jax
import jax.numpy as jnp
from jax import lax
from jax.experimental import pallas as pl
from jax.experimental.pallas import tpu as pltpu
from jax.sharding import PartitionSpec as P

BLK = 64
EPS = 1e-05
CHUNKS = 4
LIMIT = 58 * 1024 * 1024
MESH = pl.DeviceIdType.MESH
NT = (((1,), (1,)), ((), ()))
F32 = jnp.float32
BF16 = jnp.bfloat16


def greet(here, sections):
    barrier = pltpu.get_barrier_semaphore()
    right = lax.rem(here + 1, sections)
    left = lax.rem(here + sections - 1, sections)
    for side in (left, right):
        pl.semaphore_signal(barrier, inc=1, device_id={"section": side}, device_id_type=MESH)
    pl.semaphore_wait(barrier, 2)
    return left, right


def mask_up(wa, lap, rows_a):
    def body(b, _):
        rows = pl.ds(pl.multiple_of(b * BLK, BLK), BLK)
        keep = rows_a[lap, pl.ds(b, 1), :].astype(BF16)
        wa[lap, rows, :] = wa[lap, rows, :] * keep
        return 0

    lax.fori_loop(0, wa.shape[1] // BLK, body, 0)


def mask_down(wb, lap, cols_b):
    def body(b, _):
        rows = pl.ds(pl.multiple_of(b * BLK, BLK), BLK)
        keep = cols_b[lap, pl.ds(b, 1), :].astype(BF16)
        wb[lap, rows, :] = wb[lap, rows, :] * keep
        return 0

    lax.fori_loop(0, wb.shape[1] // BLK, body, 0)


def chunk_copies(src, dst, sems, base):
    wide = src.shape[-1] // CHUNKS
    return [
        pltpu.make_async_copy(src.at[:, :, pl.ds(c * wide, wide)], dst.at[:, c], sems.at[base + c])
        for c in range(CHUNKS)
    ]


def forward_items(here, sections, right, wa, wb, xs, xout, ps, invs, send, recv):
    batches = xs.shape[0] // 2
    wide = xs.shape[-1]
    width = wide * CHUNKS

    def hop(i, c):
        last = here == sections - 1
        slot = jnp.minimum(i + jnp.where(last, batches, 0), 2 * batches - 1)
        return pltpu.make_async_remote_copy(
            src_ref=xout.at[i, c],
            dst_ref=xs.at[slot, c],
            send_sem=send.at[i, c],
            recv_sem=recv.at[slot, c],
            device_id={"section": right},
            device_id_type=MESH,
        )

    def landed(i, c):
        return pltpu.make_async_remote_copy(
            src_ref=xout.at[i, c],
            dst_ref=xs.at[i, c],
            send_sem=send.at[i, c],
            recv_sem=recv.at[i, c],
            device_id={"section": right},
            device_id_type=MESH,
        )

    def item(i, _):
        lap = i // batches
        from_left = (here > 0) | (lap > 0)
        go_on = (here < sections - 1) | (lap == 0)
        total = None
        square = None
        for c in range(CHUNKS):

            @pl.when(from_left)
            def _():
                landed(i, c).wait_recv()

            x = xs[i, c]
            xf = x.astype(F32)
            sq = jnp.sum(xf * xf, axis=-1, keepdims=True)
            q = jnp.dot(x, wa[lap, pl.ds(c * wide, wide), :], preferred_element_type=F32)
            total = q if total is None else total + q
            square = sq if square is None else square + sq
        inv = lax.rsqrt(square / width + EPS)
        p = total * inv
        ps[i] = p
        invs[i] = jnp.broadcast_to(inv, invs.shape[1:])

        @pl.when(go_on)
        def _():
            h = (p * jax.nn.sigmoid(p)).astype(BF16)
            for c in range(CHUNKS):
                y = jnp.dot(h, wb[lap, :, pl.ds(c * wide, wide)], preferred_element_type=F32)
                xout[i, c] = (xs[i, c].astype(F32) + y).astype(BF16)
                hop(i, c).start()

        return 0

    lax.fori_loop(0, 2 * batches, item, 0)

    def finish():
        def body(i, _):
            lap = i // batches

            @pl.when((here < sections - 1) | (lap == 0))
            def _():
                for c in range(CHUNKS):
                    hop(i, c).wait_send()

            return 0

        lax.fori_loop(0, 2 * batches, body, 0)

    return finish


def backward_items(here, sections, left, lap, base, wa, wb, xs, ps, invs, gs, gout, gpis, hs, send, recv, gnext, nsend, nrecv):
    batches = gs.shape[0]
    wide = gs.shape[-1]
    width = wide * CHUNKS

    def hop(i, c):
        return pltpu.make_async_remote_copy(
            src_ref=gout.at[i, c],
            dst_ref=gs.at[i, c],
            send_sem=send.at[i, c],
            recv_sem=recv.at[i, c],
            device_id={"section": left},
            device_id_type=MESH,
        )

    def wrap(i, c):
        return pltpu.make_async_remote_copy(
            src_ref=gout.at[i, c],
            dst_ref=gnext.at[i, c],
            send_sem=nsend.at[i, c],
            recv_sem=nrecv.at[i, c],
            device_id={"section": left},
            device_id_type=MESH,
        )

    def item(i, _):
        total = None
        for c in range(CHUNKS):

            @pl.when(here < sections - 1)
            def _():
                hop(i, c).wait_recv()

            q = lax.dot_general(
                gs[i, c], wb[lap, :, pl.ds(c * wide, wide)], NT, preferred_element_type=F32
            )
            total = q if total is None else total + q
        p = ps[base + i]
        inv = invs[base + i][:, :1]
        sg = jax.nn.sigmoid(p)
        gp = total * sg * (1.0 + p * (1.0 - sg))
        rounded = gp.astype(BF16)
        gpis[i] = gp * inv
        hs[i] = p * sg
        mean = jnp.sum(rounded.astype(F32) * p, axis=-1, keepdims=True) / width
        scale = inv * inv * mean

        def outgoing():
            for c in range(CHUNKS):
                gn = lax.dot_general(
                    rounded, wa[lap, pl.ds(c * wide, wide), :], NT, preferred_element_type=F32
                )
                out = gs[i, c].astype(F32) + inv * gn - xs[base + i, c].astype(F32) * scale
                gout[i, c] = out.astype(BF16)

                @pl.when(here > 0)
                def _():
                    hop(i, c).start()

                if gnext is not None:

                    @pl.when(here == 0)
                    def _():
                        wrap(i, c).start()

        if gnext is not None:
            outgoing()
        else:
            pl.when(here > 0)(outgoing)
        return 0

    def finish():
        def body(i, _):
            for c in range(CHUNKS):

                @pl.when(here > 0)
                def _():
                    hop(i, c).wait_send()

                if gnext is not None:

                    @pl.when(here == 0)
                    def _():
                        wrap(i, c).wait_send()

                    @pl.when(here == sections - 1)
                    def _():
                        wrap(i, c).wait_recv()

            return 0

        lax.fori_loop(0, batches, body, 0)

    return item, finish


def weight_terms(base, xs, gs, gpis, hs, turned, stage):
    batches = gs.shape[0]
    wide = gs.shape[-1]
    tokens = gs.shape[2]
    rows = batches * tokens
    groups, inner, span = stage.shape[1:]
    flat_gp = gpis[...].reshape(rows, inner)
    flat_h = hs[...].reshape(rows, inner)
    turned[0] = jnp.transpose(flat_gp).astype(BF16)
    turned[1] = jnp.transpose(flat_h).astype(BF16)
    per = wide // span

    def owner(c, _):
        for k in range(per):
            q = c * per + k
            cols = pl.ds(k * span, span)
            x = xs[pl.ds(base, batches), c, :, cols].reshape(rows, span)
            g = gs[:, c, :, cols].reshape(rows, span)
            stage[0, q] = jnp.dot(turned[0], x, preferred_element_type=F32).astype(BF16)
            stage[1, q] = jnp.dot(turned[1], g, preferred_element_type=F32).astype(BF16)
        return 0

    lax.fori_loop(0, CHUNKS, owner, 0)


def ring(me, groups, stage, slots, sends, recvs):
    half = stage.shape[2] // 2
    place = jnp.where(me % 2 == 0, me // 2, groups - 1 - me // 2)

    def device_at(spot):
        return jnp.where(spot < groups // 2, 2 * spot, 2 * (groups - 1 - spot) + 1)

    def peer(way):
        return device_at(lax.rem(place + (1 if way == 0 else groups - 1), groups))

    def own(way, part, k):
        spot = place + 2 * groups - 1 - k if way == 0 else place + 1 + k
        return stage.at[part, device_at(lax.rem(spot, groups)), pl.ds(way * half, half)]

    def hop(way, part, k):
        return pltpu.make_async_remote_copy(
            src_ref=slots.at[way, jnp.maximum(k - 1, 0), part],
            dst_ref=slots.at[way, k, part],
            send_sem=sends.at[way, k, part],
            recv_sem=recvs.at[way, k, part],
            device_id={"dp": peer(way)},
            device_id_type=MESH,
        )

    def first(way, part):
        return pltpu.make_async_remote_copy(
            src_ref=own(way, part, 0),
            dst_ref=slots.at[way, 0, part],
            send_sem=sends.at[way, 0, part],
            recv_sem=recvs.at[way, 0, part],
            device_id={"dp": peer(way)},
            device_id_type=MESH,
        )

    pairs = [(way, part) for part in range(2) for way in range(2)]

    def begin():
        for way, part in pairs:
            first(way, part).start()

    def step(k):
        for way, part in pairs:
            hop(way, part, k - 1).wait_recv()
            term = own(way, part, k)[...].astype(F32)
            slot = slots.at[way, k - 1, part]
            slot[...] = (slot[...].astype(F32) + term).astype(BF16)
            hop(way, part, k).start()

    def end(total):
        for way, part in pairs:
            hop(way, part, groups - 2).wait_recv()
            term = own(way, part, groups - 1)[...].astype(F32)
            total[part, pl.ds(way * half, half)] = (
                slots[way, groups - 2, part].astype(F32) + term
            )

    def drain():
        for way, part in pairs:
            first(way, part).wait_send()

        def body(k, _):
            for way, part in pairs:
                hop(way, part, k).wait_send()
            return 0

        lax.fori_loop(1, groups - 1, body, 0)

    return begin, step, end, drain


def first_kernel(
    sections, micro, cot, weight_a, weight_b, rows_a, cols_b,
    out, x_keep, p_keep, inv_keep, g_keep,
    wa, wb, xs, xout, ps, invs, gs, gout, gnext, gpis, hs, turned, stage,
    load, keep, xsend, xrecv, gsend, grecv, nsend, nrecv, out_sem,
):
    here = lax.axis_index("section")
    batches = gs.shape[0]
    loads = []
    for lap in range(2):
        loads.append(pltpu.make_async_copy(weight_a.at[lap, 0], wa.at[lap], load.at[2 * lap]))
        loads.append(pltpu.make_async_copy(weight_b.at[lap, 0], wb.at[lap], load.at[2 * lap + 1]))
    for copy in loads:
        copy.start()
    x_in = chunk_copies(micro, xs.at[pl.ds(0, batches)], load, 4)
    g_in = chunk_copies(cot, gs, load, 4 + CHUNKS)

    @pl.when(here == 0)
    def _():
        for copy in x_in:
            copy.start()

    @pl.when(here == sections - 1)
    def _():
        for copy in g_in:
            copy.start()

    left, right = greet(here, sections)
    for lap in range(2):
        loads[2 * lap].wait()
        mask_up(wa, lap, rows_a)
        loads[2 * lap + 1].wait()
        mask_down(wb, lap, cols_b)

    @pl.when(here == 0)
    def _():
        for copy in x_in:
            copy.wait()

    x_done = forward_items(here, sections, right, wa, wb, xs, xout, ps, invs, xsend, xrecv)

    @pl.when(here == sections - 1)
    def _():
        for copy in g_in:
            copy.wait()

    keeps = [
        pltpu.make_async_copy(xs.at[pl.ds(0, batches)], x_keep, keep.at[0]),
        pltpu.make_async_copy(ps.at[pl.ds(0, batches)], p_keep, keep.at[1]),
        pltpu.make_async_copy(invs.at[pl.ds(0, batches)], inv_keep, keep.at[2]),
    ]
    for copy in keeps:
        copy.start()
    item, g_done = backward_items(
        here, sections, left, 1, batches, wa, wb, xs, ps, invs, gs, gout, gpis, hs, gsend, grecv, gnext, nsend, nrecv
    )
    lax.fori_loop(0, batches, item, 0)
    weight_terms(batches, xs, gs, gpis, hs, turned, stage)
    outs = [pltpu.make_async_copy(stage, out, out_sem.at[0])]
    outs[0].start()
    x_done()
    g_done()

    @pl.when(here == sections - 1)
    def _():
        copy = pltpu.make_async_copy(gnext, g_keep, keep.at[3])
        copy.start()
        copy.wait()

    for copy in keeps + outs:
        copy.wait()


def second_kernel(
    sections, groups, term_one, x_keep, p_keep, inv_keep, g_keep, weight_a, weight_b, rows_a, cols_b,
    out,
    wa, wb, xs, ps, invs, gs, gout, gpis, hs, turned, stage, later, slots, late_slots, totals,
    load, gsend, grecv, rsend, rrecv, late_send, late_recv, out_sem,
):
    here = lax.axis_index("section")
    me = lax.axis_index("dp")
    batches = gs.shape[0]
    term_in = pltpu.make_async_copy(term_one, later, load.at[6])
    term_in.start()
    loads = [
        pltpu.make_async_copy(weight_b.at[0, 0], wb.at[0], load.at[1]),
        pltpu.make_async_copy(weight_a.at[0, 0], wa.at[0], load.at[0]),
        pltpu.make_async_copy(x_keep, xs, load.at[2]),
        pltpu.make_async_copy(p_keep, ps, load.at[3]),
        pltpu.make_async_copy(inv_keep, invs, load.at[4]),
    ]
    for copy in loads:
        copy.start()
    g_in = pltpu.make_async_copy(g_keep, gs, load.at[5])

    @pl.when(here == sections - 1)
    def _():
        g_in.start()

    barrier = pltpu.get_barrier_semaphore()
    place = jnp.where(me % 2 == 0, me // 2, groups - 1 - me // 2)
    left = lax.rem(here + sections - 1, sections)
    for away in (1, groups - 1):
        spot = lax.rem(place + away, groups)
        other = jnp.where(spot < groups // 2, 2 * spot, 2 * (groups - 1 - spot) + 1)
        pl.semaphore_signal(barrier, inc=1, device_id={"dp": other}, device_id_type=MESH)
    for away in (1, sections - 1):
        other = lax.rem(here + away, sections)
        pl.semaphore_signal(barrier, inc=1, device_id={"section": other}, device_id_type=MESH)
    pl.semaphore_wait(barrier, 4)
    late_begin, late_step, late_end, late_drain = ring(
        me, groups, later, late_slots, late_send, late_recv
    )
    begin, step, end, drain = ring(me, groups, stage, slots, rsend, rrecv)
    term_in.wait()
    late_begin()
    for copy in loads:
        copy.wait()
    mask_down(wb, 0, cols_b)
    mask_up(wa, 0, rows_a)

    @pl.when(here == sections - 1)
    def _():
        g_in.wait()

    item, g_done = backward_items(
        here, sections, left, 0, 0, wa, wb, xs, ps, invs, gs, gout, gpis, hs, gsend, grecv, None, None, None
    )
    turns = batches + sections - 1

    def turn(t, _):
        i = t - (sections - 1 - here)

        @pl.when((i >= 0) & (i < batches))
        def _():
            item(jnp.clip(i, 0, batches - 1), 0)

        @pl.when(t + 1 <= groups - 2)
        def _():
            late_step(jnp.minimum(t + 1, groups - 2))

        return 0

    lax.fori_loop(0, turns, turn, 0)
    for k in range(turns + 1, groups - 1):
        late_step(jnp.int32(k))
    weight_terms(0, xs, gs, gpis, hs, turned, stage)
    begin()
    late_end(totals.at[1])

    def walk(k, _):
        step(k)
        return 0

    lax.fori_loop(1, groups - 1, walk, 0)
    end(totals.at[0])
    copy = pltpu.make_async_copy(totals, out, out_sem.at[0])
    copy.start()
    g_done()
    late_drain()
    drain()
    copy.wait()


def expand_blocks(mask):
    return jnp.repeat(jnp.repeat(mask, BLK, axis=-2), BLK, axis=-1)


def on_device(micro_inputs, out_cotangent, weight_a, weight_b, mask_a, mask_b):
    sections = lax.axis_size("section")
    groups = lax.axis_size("dp")
    owner = lax.axis_index("dp")
    batches, tokens, width = micro_inputs.shape
    inner = weight_a.shape[3]
    span = width // groups
    wide = width // CHUNKS
    rows_a = jnp.repeat(mask_a[:, 0].astype(F32), BLK, axis=-1)
    cols_b = jnp.repeat(mask_b[:, 0].astype(F32), BLK, axis=-1)
    any_spec = pl.BlockSpec(memory_space=pl.ANY)
    vmem_spec = pl.BlockSpec(memory_space=pltpu.VMEM)
    dma = pltpu.SemaphoreType.DMA
    term = jax.ShapeDtypeStruct((2, groups, inner, span), BF16)
    block = (batches, CHUNKS, tokens, wide)
    flops = 2 * batches * tokens * width * inner

    def call(kernel, cid, in_specs, outs, scratch, count):
        return pl.pallas_call(
            kernel,
            out_shape=outs,
            in_specs=in_specs,
            out_specs=tuple(any_spec for _ in outs),
            scratch_shapes=scratch,
            compiler_params=pltpu.CompilerParams(
                collective_id=cid, has_side_effects=True, vmem_limit_bytes=LIMIT
            ),
            cost_estimate=pl.CostEstimate(
                flops=count * flops, bytes_accessed=40 * 1024 * 1024, transcendentals=0
            ),
        )

    term_one, x0, p0, inv0, g0 = call(
        functools.partial(first_kernel, sections),
        0,
        [any_spec] * 4 + [vmem_spec] * 2,
        (
            term,
            jax.ShapeDtypeStruct(block, BF16),
            jax.ShapeDtypeStruct((batches, tokens, inner), F32),
            jax.ShapeDtypeStruct((batches, tokens, 128), F32),
            jax.ShapeDtypeStruct(block, BF16),
        ),
        [
            pltpu.VMEM((2, width, inner), BF16),
            pltpu.VMEM((2, inner, width), BF16),
            pltpu.VMEM((2 * batches,) + block[1:], BF16),
            pltpu.VMEM((2 * batches,) + block[1:], BF16),
            pltpu.VMEM((2 * batches, tokens, inner), F32),
            pltpu.VMEM((2 * batches, tokens, 128), F32),
            pltpu.VMEM(block, BF16),
            pltpu.VMEM(block, BF16),
            pltpu.VMEM(block, BF16),
            pltpu.VMEM((batches, tokens, inner), F32),
            pltpu.VMEM((batches, tokens, inner), F32),
            pltpu.VMEM((2, inner, batches * tokens), BF16),
            pltpu.VMEM((2, groups, inner, span), BF16),
            dma((4 + 2 * CHUNKS,)),
            dma((4,)),
            dma((2 * batches, CHUNKS)),
            dma((2 * batches, CHUNKS)),
            dma((batches, CHUNKS)),
            dma((batches, CHUNKS)),
            dma((batches, CHUNKS)),
            dma((batches, CHUNKS)),
            dma((2,)),
        ],
        8,
    )(micro_inputs, out_cotangent, weight_a, weight_b, rows_a, cols_b)

    ring_slots = (2, groups - 1, 2, inner // 2, span)
    (totals,) = call(
        functools.partial(second_kernel, sections, groups),
        1,
        [any_spec] * 7 + [vmem_spec] * 2,
        (jax.ShapeDtypeStruct((2, 2, inner, span), F32),),
        [
            pltpu.VMEM((1, width, inner), BF16),
            pltpu.VMEM((1, inner, width), BF16),
            pltpu.VMEM(block, BF16),
            pltpu.VMEM((batches, tokens, inner), F32),
            pltpu.VMEM((batches, tokens, 128), F32),
            pltpu.VMEM(block, BF16),
            pltpu.VMEM(block, BF16),
            pltpu.VMEM((batches, tokens, inner), F32),
            pltpu.VMEM((batches, tokens, inner), F32),
            pltpu.VMEM((2, inner, batches * tokens), BF16),
            pltpu.VMEM((2, groups, inner, span), BF16),
            pltpu.VMEM((2, groups, inner, span), BF16),
            pltpu.VMEM(ring_slots, BF16),
            pltpu.VMEM(ring_slots, BF16),
            pltpu.VMEM((2, 2, inner, span), F32),
            dma((7,)),
            dma((batches, CHUNKS)),
            dma((batches, CHUNKS)),
            dma(ring_slots[:3]),
            dma(ring_slots[:3]),
            dma(ring_slots[:3]),
            dma(ring_slots[:3]),
            dma((1,)),
        ],
        4,
    )(term_one, x0, p0, inv0, g0, weight_a, weight_b, rows_a, cols_b)

    def settle(lap):
        held = span // BLK
        own_a = expand_blocks(lax.dynamic_slice_in_dim(mask_a[lap, 0], owner * held, held, 0))
        own_b = expand_blocks(lax.dynamic_slice_in_dim(mask_b[lap, 0], owner * held, held, 1))
        return jnp.transpose(totals[lap, 0]) * own_a.astype(F32), totals[lap, 1] * own_b.astype(F32)

    later_zero = settle(0)
    later_one = settle(1)
    grad_a = jnp.stack([later_zero[0], later_one[0]])[:, None]
    grad_b = jnp.stack([later_zero[1], later_one[1]])[:, None]
    return (grad_a, grad_b)


def solution(mesh):
    placed = (
        P(None, "dp", None),
        P(None, "dp", None),
        P(None, "section", None, None),
        P(None, "section", None, None),
        P(None, "section", None, None),
        P(None, "section", None, None),
    )
    return jax.shard_map(
        on_device,
        mesh=mesh,
        in_specs=placed,
        out_specs=(P(None, "section", "dp", None), P(None, "section", None, "dp")),
        check_vma=False,
    )
```

profile of v0, /device:TPU:0, one launch (start us, length us, event | category | flops | bytes accessed | tf_op | source)
XLA Modules:
  0.0 284.1 jit_solution(9446002522115791990)
XLA Ops:
  0.6 0.7 convert_bitcast_fusion.1
  1.3 0.1 copy.15
  1.4 0.2 broadcast_in_dim.36
  1.6 0.9 reshape.76.rows_a
  2.5 0.7 convert_bitcast_fusion
  3.2 0.2 broadcast_in_dim.37
  3.4 0.9 reshape.77.cols_b
  4.3 104.1 %shard_map.77 = (bf16[2,8,512,512]{3,2,1,0:T(8,128)(2,1)}, bf16[4,4,64,1024]{3,2,1,0:T(8,128)(2,1)}, f32[4,64,512]{2,1,0:T(8,128)}, f32[4,64,128]{2,1,0:T(8,128)}, bf16[4,4,64,1024]{3,2,1,0:T(8,128)(2,1)}) custom-call(bf16[4,64,4096]{2,1,0:T(8,128)(2,1)} %micro.1, bf16[4,64,4096]{2,1,0:T(8,128)(2,1)} %cot.1, bf16[2,1,4096,512]{3,2,1,0:T(8,128)(2,1)} %weight_a.3, ...), custom_call_target="tpu_custom_call" | custom-call | flops 8589934592 | bytes 41943040 | tf_op jit(solution)/shard_map/pallas_call | solution.py:527
  108.4 166.1 %shard_map.78 = f32[2,2,512,512]{3,2,1,0:T(8,128)} custom-call(bf16[2,8,512,512]{3,2,1,0:T(8,128)(2,1)} %get-tuple-element.7.term_one, bf16[4,4,64,1024]{3,2,1,0:T(8,128)(2,1)} %get-tuple-element.8.x_keep, f32[4,64,512]{2,1,0:T(8,128)} %get-tuple-element.9.p_keep, f32[4,64,128]{2,1,0:T(8,128)} %get-tuple-element.10.inv_keep, ...), custom_call_target="tpu_custom_call" | custom-call | flops 4294967296 | bytes 41943040 | tf_op jit(solution)/shard_map/pallas_call | solution.py:566
  274.6 0.1 convert_bitcast_fusion.2
  274.7 0.1 copy.20
  274.7 0.1 broadcast_in_dim.43
  274.8 0.1 convert_element_type.96
  274.9 0.1 broadcast_in_dim.44
  275.0 0.3 copy.21
  275.4 0.1 broadcast_in_dim.45
  275.5 0.1 convert_element_type.100
  275.6 0.1 broadcast_in_dim.46
  275.7 0.3 copy.23
  276.1 2.0 bitcast_multiply_fusion.3
  278.1 1.5 maximum_bitcast_fusion.1
  279.6 0.1 constant_dynamic-slice_fusion
  279.7 0.1 copy.26
  279.7 0.1 copy.17
  279.8 0.1 broadcast_in_dim.38
  279.9 0.1 convert_element_type.88
  280.0 0.1 copy.19
  280.1 0.1 broadcast_in_dim.40
  280.2 0.1 convert_element_type.92
  280.3 1.8 fusion.1
  282.1 0.2 maximum_bitcast_fusion
  282.2 1.8 copy.24
  (10 shorter events, 0.2 us)
Async XLA Ops:
  108.4 166.1 %copy-start = (s32[2,1,8,64]{3,2,1,0:T(8,128)S(1)}, s32[2,1,8,64]{3,2,1,0:T(8,128)}, u32[]{:S(2)}) copy-start(s32[2,1,8,64]{3,2,1,0:T(8,128)} %param.11) | copy-start | bytes 12292
  278.1 1.5 copy-start.1
where the time goes:
time: 284 us
  Pallas kernels  270 us (95%)
  other arithmetic  6.97 us (2%)
  local copies, waits for them, and re-layouts  6.1 us (2%)
    pallas_call x1, Pallas kernels, on_device(): call(functools.partial(second_kernel, sections, groups), 1, [any_spec] *...  166 us
    pallas_call x1, Pallas kernels, on_device(): call(functools.partial(first_kernel, sections), 0, [any_spec] * 4 + [vmem...  104 us

commit v1 on v0

v1 whole, which is shorter than its diff:
```python
import functools

import jax
import jax.numpy as jnp
from jax import lax
from jax.experimental import pallas as pl
from jax.experimental.pallas import tpu as pltpu
from jax.sharding import PartitionSpec as P

BLK = 64
EPS = 1e-05
CHUNKS = 4
LIMIT = 64 * 1024 * 1024 - 64 * 1024
MESH = pl.DeviceIdType.MESH
NT = (((1,), (1,)), ((), ()))
F32 = jnp.float32
BF16 = jnp.bfloat16


def mask_up(wa, lap, rows_a):
    def body(b, _):
        rows = pl.ds(pl.multiple_of(b * BLK, BLK), BLK)
        keep = rows_a[lap, pl.ds(b, 1), :].astype(BF16)
        wa[lap, rows, :] = wa[lap, rows, :] * keep
        return 0

    lax.fori_loop(0, wa.shape[1] // BLK, body, 0)


def mask_down(wb, lap, cols_b):
    def body(b, _):
        rows = pl.ds(pl.multiple_of(b * BLK, BLK), BLK)
        keep = cols_b[lap, pl.ds(b, 1), :].astype(BF16)
        wb[lap, rows, :] = wb[lap, rows, :] * keep
        return 0

    lax.fori_loop(0, wb.shape[1] // BLK, body, 0)


def chunk_copies(src, dst, sems, base):
    wide = src.shape[-1] // CHUNKS
    return [
        pltpu.make_async_copy(src.at[:, :, pl.ds(c * wide, wide)], dst.at[:, c], sems.at[base + c])
        for c in range(CHUNKS)
    ]


def forward_items(here, sections, right, prepare, wa, wb, xs, xout, ps, invs, send, recv):
    batches = xs.shape[0] // 2
    wide = xs.shape[-1]
    width = wide * CHUNKS

    def hop(i, c):
        last = here == sections - 1
        slot = jnp.minimum(i + jnp.where(last, batches, 0), 2 * batches - 1)
        return pltpu.make_async_remote_copy(
            src_ref=xout.at[i, c],
            dst_ref=xs.at[slot, c],
            send_sem=send.at[i, c],
            recv_sem=recv.at[slot, c],
            device_id={"section": right},
            device_id_type=MESH,
        )

    def landed(i, c):
        return pltpu.make_async_remote_copy(
            src_ref=xout.at[i, c],
            dst_ref=xs.at[i, c],
            send_sem=send.at[i, c],
            recv_sem=recv.at[i, c],
            device_id={"section": right},
            device_id_type=MESH,
        )

    def item(i, _):
        lap = i // batches
        from_left = (here > 0) | (lap > 0)
        go_on = (here < sections - 1) | (lap == 0)

        @pl.when((here == 0) & (i == batches))
        def _():
            prepare()

        total = None
        square = None
        for c in range(CHUNKS):

            @pl.when(from_left)
            def _():
                landed(i, c).wait_recv()

            x = xs[i, c]
            xf = x.astype(F32)
            sq = jnp.sum(xf * xf, axis=-1, keepdims=True)
            q = jnp.dot(x, wa[lap, pl.ds(c * wide, wide), :], preferred_element_type=F32)
            total = q if total is None else total + q
            square = sq if square is None else square + sq
        inv = lax.rsqrt(square / width + EPS)
        p = total * inv
        ps[i] = p
        invs[i] = jnp.broadcast_to(inv, invs.shape[1:])

        @pl.when(go_on)
        def _():
            h = (p * jax.nn.sigmoid(p)).astype(BF16)
            for c in range(CHUNKS):
                y = jnp.dot(h, wb[lap, :, pl.ds(c * wide, wide)], preferred_element_type=F32)
                xout[i, c] = (xs[i, c].astype(F32) + y).astype(BF16)
                hop(i, c).start()

        return 0

    lax.fori_loop(0, 2 * batches, item, 0)

    def finish():
        def body(i, _):
            lap = i // batches

            @pl.when((here < sections - 1) | (lap == 0))
            def _():
                for c in range(CHUNKS):
                    hop(i, c).wait_send()

            return 0

        lax.fori_loop(0, 2 * batches, body, 0)

    return finish


def backward_items(here, sections, left, lap, wa, wb, xs, ps, invs, gs, gout, gpis, hs, send, recv):
    batches = gpis.shape[0]
    wide = gs.shape[-1]
    width = wide * CHUNKS
    base = lap * batches

    def hop(i, c):
        slot = base + i
        if lap:
            slot = slot - jnp.where(here == 0, batches, 0)
        return pltpu.make_async_remote_copy(
            src_ref=gout.at[base + i, c],
            dst_ref=gs.at[slot, c],
            send_sem=send.at[base + i, c],
            recv_sem=recv.at[slot, c],
            device_id={"section": left},
            device_id_type=MESH,
        )

    def landed(i, c):
        return pltpu.make_async_remote_copy(
            src_ref=gout.at[base + i, c],
            dst_ref=gs.at[base + i, c],
            send_sem=send.at[base + i, c],
            recv_sem=recv.at[base + i, c],
            device_id={"section": left},
            device_id_type=MESH,
        )

    def item(i, _):
        total = None
        for c in range(CHUNKS):
            if lap:

                @pl.when(here < sections - 1)
                def _():
                    landed(i, c).wait_recv()

            else:
                landed(i, c).wait_recv()
            q = lax.dot_general(
                gs[base + i, c], wb[lap, :, pl.ds(c * wide, wide)], NT, preferred_element_type=F32
            )
            total = q if total is None else total + q
        p = ps[base + i]
        inv = invs[base + i][:, :1]
        sg = jax.nn.sigmoid(p)
        gp = total * sg * (1.0 + p * (1.0 - sg))
        rounded = gp.astype(BF16)
        gpis[i] = (gp * inv).astype(BF16)
        hs[i] = (p * sg).astype(BF16)
        mean = jnp.sum(rounded.astype(F32) * p, axis=-1, keepdims=True) / width
        scale = inv * inv * mean

        def outgoing():
            for c in range(CHUNKS):
                gn = lax.dot_general(
                    rounded, wa[lap, pl.ds(c * wide, wide), :], NT, preferred_element_type=F32
                )
                out = gs[base + i, c].astype(F32) + inv * gn - xs[base + i, c].astype(F32) * scale
                gout[base + i, c] = out.astype(BF16)
                hop(i, c).start()

        if lap:
            outgoing()
        else:
            pl.when(here > 0)(outgoing)
        return 0

    def finish():
        def body(i, _):
            for c in range(CHUNKS):
                if lap:
                    hop(i, c).wait_send()
                else:

                    @pl.when(here > 0)
                    def _():
                        hop(i, c).wait_send()

            return 0

        lax.fori_loop(0, batches, body, 0)

    return item, finish


def weight_terms(base, xs, gs, gpis, hs, turned, stage):
    batches = gpis.shape[0]
    wide = gs.shape[-1]
    tokens = gs.shape[2]
    rows = batches * tokens
    groups, inner, span = stage.shape[1:]
    per = wide // span
    for part, (left, right) in enumerate(((gpis, xs), (hs, gs))):
        turned[...] = jnp.transpose(left[...].astype(F32).reshape(rows, inner)).astype(BF16)

        def owner(c, _):
            for k in range(per):
                block = right[pl.ds(base, batches), c, :, pl.ds(k * span, span)].reshape(rows, span)
                stage[part, c * per + k] = jnp.dot(
                    turned[...], block, preferred_element_type=F32
                ).astype(BF16)
            return 0

        lax.fori_loop(0, CHUNKS, owner, 0)


def ring(me, groups, stage, slots, sends, recvs):
    half = stage.shape[2] // 2
    place = jnp.where(me % 2 == 0, me // 2, groups - 1 - me // 2)

    def device_at(spot):
        return jnp.where(spot < groups // 2, 2 * spot, 2 * (groups - 1 - spot) + 1)

    def peer(way):
        return device_at(lax.rem(place + (1 if way == 0 else groups - 1), groups))

    def own(way, part, k):
        spot = place + 2 * groups - 1 - k if way == 0 else place + 1 + k
        return stage.at[part, device_at(lax.rem(spot, groups)), pl.ds(way * half, half)]

    def hop(way, part, k):
        return pltpu.make_async_remote_copy(
            src_ref=slots.at[way, jnp.maximum(k - 1, 0), part],
            dst_ref=slots.at[way, k, part],
            send_sem=sends.at[way, k, part],
            recv_sem=recvs.at[way, k, part],
            device_id={"dp": peer(way)},
            device_id_type=MESH,
        )

    def first(way, part):
        return pltpu.make_async_remote_copy(
            src_ref=own(way, part, 0),
            dst_ref=slots.at[way, 0, part],
            send_sem=sends.at[way, 0, part],
            recv_sem=recvs.at[way, 0, part],
            device_id={"dp": peer(way)},
            device_id_type=MESH,
        )

    pairs = [(way, part) for part in range(2) for way in range(2)]

    def begin():
        for way, part in pairs:
            first(way, part).start()

    def step(k):
        for way, part in pairs:
            hop(way, part, k - 1).wait_recv()
            term = own(way, part, k)[...].astype(F32)
            slot = slots.at[way, k - 1, part]
            slot[...] = (slot[...].astype(F32) + term).astype(BF16)
            hop(way, part, k).start()

    def end(total):
        for way, part in pairs:
            hop(way, part, groups - 2).wait_recv()
            term = own(way, part, groups - 1)[...].astype(F32)
            total[part, pl.ds(way * half, half)] = (
                slots[way, groups - 2, part].astype(F32) + term
            )

    def drain():
        for way, part in pairs:
            first(way, part).wait_send()

        def body(k, _):
            for way, part in pairs:
                hop(way, part, k).wait_send()
            return 0

        lax.fori_loop(1, groups - 1, body, 0)

    return begin, step, end, drain


def whole_kernel(
    sections, groups, micro, cot, weight_a, weight_b, rows_a, cols_b,
    out,
    wa, wb, xs, xout, ps, invs, gs, gpis, hs, turned, stage, later, slots, late_slots, totals,
    load, xsend, xrecv, gsend, grecv, rsend, rrecv, late_send, late_recv, out_sem,
):
    here = lax.axis_index("section")
    me = lax.axis_index("dp")
    batches = gpis.shape[0]
    loads = []
    for lap in range(2):
        loads.append(pltpu.make_async_copy(weight_a.at[lap, 0], wa.at[lap], load.at[2 * lap]))
        loads.append(pltpu.make_async_copy(weight_b.at[lap, 0], wb.at[lap], load.at[2 * lap + 1]))
    x_in = chunk_copies(micro, xs.at[pl.ds(0, batches)], load, 4)
    g_in = chunk_copies(cot, gs.at[pl.ds(batches, batches)], load, 4 + CHUNKS)
    loads[0].start()

    @pl.when(here == 0)
    def _():
        for copy in x_in:
            copy.start()

    for copy in loads[1:]:
        copy.start()

    @pl.when(here == sections - 1)
    def _():
        for copy in g_in:
            copy.start()

    barrier = pltpu.get_barrier_semaphore()
    place = jnp.where(me % 2 == 0, me // 2, groups - 1 - me // 2)
    right = lax.rem(here + 1, sections)
    left = lax.rem(here + sections - 1, sections)
    for away in (1, groups - 1):
        spot = lax.rem(place + away, groups)
        other = jnp.where(spot < groups // 2, 2 * spot, 2 * (groups - 1 - spot) + 1)
        pl.semaphore_signal(barrier, inc=1, device_id={"dp": other}, device_id_type=MESH)
    for other in (left, right):
        pl.semaphore_signal(barrier, inc=1, device_id={"section": other}, device_id_type=MESH)
    pl.semaphore_wait(barrier, 4)

    def prepare(lap):
        loads[2 * lap].wait()
        mask_up(wa, lap, rows_a)
        loads[2 * lap + 1].wait()
        mask_down(wb, lap, cols_b)

    prepare(0)

    @pl.when(here > 0)
    def _():
        prepare(1)

    @pl.when(here == 0)
    def _():
        for copy in x_in:
            copy.wait()

    x_done = forward_items(
        here, sections, right, lambda: prepare(1), wa, wb, xs, xout, ps, invs, xsend, xrecv
    )

    @pl.when(here == sections - 1)
    def _():
        for copy in g_in:
            copy.wait()

    x_done()
    late_item, late_done = backward_items(
        here, sections, left, 1, wa, wb, xs, ps, invs, gs, xout, gpis, hs, gsend, grecv
    )
    lax.fori_loop(0, batches, late_item, 0)
    weight_terms(batches, xs, gs, gpis, hs, turned, later)
    late_begin, late_step, late_end, late_drain = ring(
        me, groups, later, late_slots, late_send, late_recv
    )
    begin, step, end, drain = ring(me, groups, stage, slots, rsend, rrecv)
    late_begin()
    item, done = backward_items(
        here, sections, left, 0, wa, wb, xs, ps, invs, gs, xout, gpis, hs, gsend, grecv
    )
    turns = batches + sections - 1

    def turn(t, _):
        i = t - (sections - 1 - here)

        @pl.when((i >= 0) & (i < batches))
        def _():
            item(jnp.clip(i, 0, batches - 1), 0)

        @pl.when(t + 1 <= groups - 2)
        def _():
            late_step(jnp.minimum(t + 1, groups - 2))

        return 0

    lax.fori_loop(0, turns, turn, 0)
    for k in range(turns + 1, groups - 1):
        late_step(jnp.int32(k))
    weight_terms(0, xs, gs, gpis, hs, turned, stage)
    begin()
    late_end(totals)
    late_out = pltpu.make_async_copy(totals, out.at[1], out_sem.at[0])
    late_out.start()

    def walk(k, _):
        step(k)
        return 0

    lax.fori_loop(1, groups - 1, walk, 0)
    late_out.wait()
    end(totals)
    last_out = pltpu.make_async_copy(totals, out.at[0], out_sem.at[1])
    last_out.start()
    late_done()
    done()
    late_drain()
    drain()
    last_out.wait()


def expand_blocks(mask):
    return jnp.repeat(jnp.repeat(mask, BLK, axis=-2), BLK, axis=-1)


def on_device(micro_inputs, out_cotangent, weight_a, weight_b, mask_a, mask_b):
    sections = lax.axis_size("section")
    groups = lax.axis_size("dp")
    owner = lax.axis_index("dp")
    batches, tokens, width = micro_inputs.shape
    inner = weight_a.shape[3]
    span = width // groups
    wide = width // CHUNKS
    rows_a = jnp.repeat(mask_a[:, 0].astype(F32), BLK, axis=-1)
    cols_b = jnp.repeat(mask_b[:, 0].astype(F32), BLK, axis=-1)
    any_spec = pl.BlockSpec(memory_space=pl.ANY)
    vmem_spec = pl.BlockSpec(memory_space=pltpu.VMEM)
    dma = pltpu.SemaphoreType.DMA
    block = (CHUNKS, tokens, wide)
    ring_slots = (2, groups - 1, 2, inner // 2, span)
    flops = 2 * batches * tokens * width * inner
    totals = pl.pallas_call(
        functools.partial(whole_kernel, sections, groups),
        out_shape=jax.ShapeDtypeStruct((2, 2, inner, span), F32),
        in_specs=[any_spec] * 4 + [vmem_spec] * 2,
        out_specs=any_spec,
        scratch_shapes=[
            pltpu.VMEM((2, width, inner), BF16),
            pltpu.VMEM((2, inner, width), BF16),
            pltpu.VMEM((2 * batches,) + block, BF16),
            pltpu.VMEM((2 * batches,) + block, BF16),
            pltpu.VMEM((2 * batches, tokens, inner), F32),
            pltpu.VMEM((2 * batches, tokens, 128), F32),
            pltpu.VMEM((2 * batches,) + block, BF16),
            pltpu.VMEM((batches, tokens, inner), BF16),
            pltpu.VMEM((batches, tokens, inner), BF16),
            pltpu.VMEM((inner, batches * tokens), BF16),
            pltpu.VMEM((2, groups, inner, span), BF16),
            pltpu.VMEM((2, groups, inner, span), BF16),
            pltpu.VMEM(ring_slots, BF16),
            pltpu.VMEM(ring_slots, BF16),
            pltpu.VMEM((2, inner, span), F32),
            dma((4 + 2 * CHUNKS,)),
            dma((2 * batches, CHUNKS)),
            dma((2 * batches, CHUNKS)),
            dma((2 * batches, CHUNKS)),
            dma((2 * batches, CHUNKS)),
            dma(ring_slots[:3]),
            dma(ring_slots[:3]),
            dma(ring_slots[:3]),
            dma(ring_slots[:3]),
            dma((2,)),
        ],
        compiler_params=pltpu.CompilerParams(
            collective_id=0, has_side_effects=True, vmem_limit_bytes=LIMIT
        ),
        cost_estimate=pl.CostEstimate(
            flops=12 * flops, bytes_accessed=40 * 1024 * 1024, transcendentals=0
        ),
    )(micro_inputs, out_cotangent, weight_a, weight_b, rows_a, cols_b)

    def settle(lap):
        held = span // BLK
        own_a = expand_blocks(lax.dynamic_slice_in_dim(mask_a[lap, 0], owner * held, held, 0))
        own_b = expand_blocks(lax.dynamic_slice_in_dim(mask_b[lap, 0], owner * held, held, 1))
        return jnp.transpose(totals[lap, 0]) * own_a.astype(F32), totals[lap, 1] * own_b.astype(F32)

    later_zero = settle(0)
    later_one = settle(1)
    grad_a = jnp.stack([later_zero[0], later_one[0]])[:, None]
    grad_b = jnp.stack([later_zero[1], later_one[1]])[:, None]
    return (grad_a, grad_b)


def solution(mesh):
    placed = (
        P(None, "dp", None),
        P(None, "dp", None),
        P(None, "section", None, None),
        P(None, "section", None, None),
        P(None, "section", None, None),
        P(None, "section", None, None),
    )
    return jax.shard_map(
        on_device,
        mesh=mesh,
        in_specs=placed,
        out_specs=(P(None, "section", "dp", None), P(None, "section", None, "dp")),
        check_vma=False,
    )
```

time: 284 us -> 276 us (0.972)
  Pallas kernels: 270 us -> 260 us
    pallas_call x2 -> x1, Pallas kernels: 270 us -> 260 us  [on_device(): pl.pallas_call(functools.partial(whole_kernel, sections, groups), out_sha...]
where the time goes in v1:
time: 276 us
  Pallas kernels  260 us (94%)
  local copies, waits for them, and re-layouts  8.77 us (3%)
  other arithmetic  6.2 us (2%)
    pallas_call x1, Pallas kernels, on_device(): pl.pallas_call(functools.partial(whole_kernel, sections, groups), out_sha...  260 us

profile of v1, /device:TPU:0, one launch (start us, length us, event | category | flops | bytes accessed | tf_op | source)
XLA Modules:
  0.0 276.1 jit_solution(5381721095855340605)
XLA Ops:
  0.6 0.7 fusion.2
  1.3 0.1 convert_bitcast_fusion.2
  1.4 0.1 copy.20
  1.5 0.1 broadcast_in_dim.43
  1.6 0.1 convert_element_type.96
  1.6 0.1 broadcast_in_dim.44
  1.8 1.3 copy.21
  3.1 0.1 copy.22
  3.2 0.1 broadcast_in_dim.45
  3.2 0.1 convert_element_type.100
  3.3 0.1 broadcast_in_dim.46
  3.4 1.3 copy.23
  4.8 0.1 copy.15
  4.9 0.2 broadcast_in_dim.36
  5.1 0.9 reshape.76.rows_a
  5.9 0.2 broadcast_in_dim.37
  6.1 0.9 reshape.77.cols_b
  7.0 260.4 %shard_map.77 = f32[2,2,512,512]{3,2,1,0:T(8,128)} custom-call(bf16[4,64,4096]{2,1,0:T(8,128)(2,1)} %micro.1, bf16[4,64,4096]{2,1,0:T(8,128)(2,1)} %cot.1, bf16[2,1,4096,512]{3,2,1,0:T(8,128)(2,1)} %weight_a.1, bf16[2,1,512,4096]{3,2,1,0:T(8,128)(2,1)} %weight_b.1, f32[2,64,512]{2,1,0:T(8,128)} %reshape.76.rows_a, f32[2,8,4096]{2,1,0:T(8,128)} %reshape.77.cols_b), custom_call_target="tpu_custom_call" | custom-call | flops 12884901888 | bytes 41943040 | tf_op jit(solution)/shard_map/pallas_call | solution.py:451
  267.5 2.7 bitcast_multiply_fusion.3
  270.1 1.5 maximum_bitcast_fusion.1
  271.6 0.1 constant_dynamic-slice_fusion
  271.7 0.1 copy.26
  271.8 0.1 copy.17
  271.9 0.1 broadcast_in_dim.38
  271.9 0.1 convert_element_type.88
  272.0 0.1 copy.27
  272.1 0.1 copy.19
  272.2 0.1 broadcast_in_dim.40
  272.2 0.1 convert_element_type.92
  272.3 1.8 fusion.1
  274.1 0.2 maximum_bitcast_fusion
  274.3 1.8 copy.24
  (11 shorter events, 0.0 us)
Async XLA Ops:
  3.1 1.7 copy-start.1
  3.3 2.6 copy-start
  270.1 1.5 copy-start.2
